TPU v7x, 32 devices: a whole 2x2x4 slice. The times are simulated.
32 devices in a mesh: row: 4 (over y, x), col: 8 (over z, core).
Axes of the slice: x: 2, y: 2, z: 4, core: 2. Of those that a mesh axis runs over, the one named last changes fastest.
Arguments:
- object_field: float32 [2, 1536, 2048], P(None, 'row', 'col'), may hold values from -5 to 5
- probe_modes: float32 [2, 2, 256, 256], replicated, may hold values from -4 to 4
- scan_positions: int32 [4, 8, 2, 2], P('row', 'col'), may hold values from 0 to 256, as said below
- amplitudes: bfloat16 [4, 8, 2, 256, 256], P('row', 'col'), may hold values from 0.5 to 1.5
Outputs:
- object_out: float32 [2, 1536, 2048], P(None, 'row', 'col')
- probe_out: float32 [2, 2, 256, 256], replicated
Inputs may be any that keep to these rules, and one draw needn't show every extreme that they name: `scan_positions`: in even batches the row offset is at most 128; in odd batches it is at least 192. The column offset lies in 32 to 128 in every batch. Every window lies inside its tile extended by 128 rows below and 128 columns to the right.
All inputs are finite; a program needn't handle non-finite values.
Results may differ from a plain program's by a relative error of at most 0.0003.
Values sent between devices are 32-bit elements; how exact they have to be, the bound alone decides.
A program may use at most 64 MiB of HBM per device.

v0:
```python
import functools
import math

import jax
import jax.numpy as jnp
import numpy as np
from jax import lax
from jax.experimental import pallas as pl
from jax.experimental.pallas import tpu as pltpu
from jax.sharding import PartitionSpec as P

HALO = 128
ODD_LOW = 192
F32 = jnp.float32
BF16 = jnp.bfloat16
MESH = pl.DeviceIdType.MESH


def dft_tables(width):
    index = np.arange(width)
    angle = (index[:, None] * index[None, :] % width) * (2.0 * math.pi / width)
    out = []
    for table in (np.cos(angle) / math.sqrt(width), np.sin(angle) / math.sqrt(width)):
        table = table.astype(np.float32)
        high = table.astype(BF16)
        low = (table - high.astype(np.float32)).astype(BF16)
        out += [high, low]
    return np.stack(out)


def split(value):
    high = value.astype(BF16)
    return high, (value - high.astype(F32)).astype(BF16)


def dot3(a_hi, a_lo, b_hi, b_lo):
    dot = functools.partial(jnp.dot, preferred_element_type=F32)
    return dot(a_hi, b_hi) + (dot(a_hi, b_lo) + dot(a_lo, b_hi))


def kernel(
    n_row, n_col, reduce_here, divisor,
    pos, obj, probe, amps, tables, obj_out, probe_out,
    e0, gx, n1, e1, g1, zbuf, from_left, from_right, spill1, down_send, from_up,
    a_hi, a_lo, b_hi, b_lo, xs_hi, xs_lo, ls_hi, ls_lo, fbuf, wbuf,
    sbuf, core_in, tbuf, row_in, ubuf, z_in, gather, ssem, rsem,
):
    row = lax.axis_index("row")
    col = lax.axis_index("col")
    width = probe.shape[-1]
    tile_rows, tile_cols = obj.shape[1], obj.shape[2]
    odd_own = tile_rows - ODD_LOW
    core = lax.rem(col, 2)
    zed = col // 2
    n_zed = n_col // 2
    has_left, has_right = col > 0, col < n_col - 1
    has_up, has_down = row > 0, row < n_row - 1
    partner = (row, col + 1 - 2 * core)
    row_peers = [(lax.rem(row + k, n_row), col) for k in range(1, n_row)]
    z_peers = [(row, lax.rem(zed + k, n_zed) * 2 + core) for k in range(1, n_zed)]
    left, right = (row, col - 1), (row, col + 1)
    up, down = (row - 1, col), (row + 1, col)

    count = [0]
    pending = []

    def remote(src, dst, dev, sends=None, receives=None):
        i = count[0]
        count[0] += 1
        copy = pltpu.make_async_remote_copy(
            src_ref=src, dst_ref=dst, send_sem=ssem.at[i], recv_sem=rsem.at[i],
            device_id=dev, device_id_type=MESH)

        def start():
            if sends is None:
                copy.start()
            else:
                pl.when(sends)(copy.start)
            pending.append((sends, copy))

        def arrive():
            if receives is None:
                copy.wait_recv()
            else:
                pl.when(receives)(copy.wait_recv)

        return start, arrive

    barrier = pltpu.get_barrier_semaphore()
    beside = (row, lax.rem(col + 2 * core - 1 + n_col, n_col))
    greeted = [partner, beside] + row_peers + z_peers
    for dev in greeted:
        pl.semaphore_signal(barrier, inc=1, device_id=dev, device_id_type=MESH)
    pl.semaphore_wait(barrier, len(greeted))

    halo = slice(tile_cols, tile_cols + HALO)
    start, halo_arrives = remote(obj.at[:, :, 0:HALO], e0.at[:, 0:tile_rows, halo], left, has_left, has_right)
    start()

    e0[:, 0:tile_rows, 0:tile_cols] = obj[...]
    for hi, part in ((True, 0), (False, 1)):
        cosine, sine = tables[part], tables[2 + part]
        a, b = (a_hi, b_hi) if hi else (a_lo, b_lo)
        for i in (0, 1):
            a[pl.ds(i * width, width), pl.ds(i * width, width)] = cosine
            b[pl.ds(i * width, width), pl.ds(i * width, width)] = cosine
        a[0:width, width:] = sine
        a[width:, 0:width] = -sine
        b[0:width, width:] = -sine
        b[width:, 0:width] = sine
    power = jnp.sum(
        jnp.sum(probe[0, 0] ** 2 + probe[0, 1] ** 2 + probe[1, 0] ** 2 + probe[1, 1] ** 2,
                axis=0, keepdims=True), axis=1, keepdims=True) / (width * width)
    step = 1.0 / (power + 1e-06)

    @pl.when(jnp.logical_not(has_right))
    def _():
        e0[:, 0:tile_rows, halo] = jnp.zeros((2, tile_rows, HALO), F32)
        from_right[...] = jnp.zeros_like(from_right)

    @pl.when(jnp.logical_not(has_left))
    def _():
        from_left[...] = jnp.zeros_like(from_left)
        spill1[...] = jnp.zeros_like(spill1)

    @pl.when(jnp.logical_not(has_down))
    def _():
        e1[:, odd_own : odd_own + HALO, :] = jnp.zeros((2, HALO, tile_cols + HALO), F32)

    @pl.when(jnp.logical_not(has_up))
    def _():
        from_up[...] = jnp.zeros_like(from_up)

    def block(i):
        return slice(i * width, (i + 1) * width)

    def one_hot(shape, dim, shift):
        here = lax.broadcasted_iota(jnp.int32, shape, dim)
        other = lax.broadcasted_iota(jnp.int32, shape, 1 - dim)
        return jnp.where(here == other + shift, 1.0, 0.0).astype(BF16)

    def pick(value, row_table, col_table):
        dot = functools.partial(jnp.dot, preferred_element_type=F32)
        parts = [dot(row_table, part).astype(BF16) for part in split(value)]
        return dot(parts[0], col_table) + dot(parts[1], col_table)

    def fit(source, first_row, col_start, batch, after_mode):
        height, total_lanes = source.shape[1:]
        row_table = one_hot((width, height), 1, first_row)
        col_table = one_hot((total_lanes, width), 0, col_start)
        for p in (0, 1):
            wbuf[p] = pick(source[p], row_table, col_table)
        for m in (0, 1):
            pr, pi, wr, wi = probe[m, 0], probe[m, 1], wbuf[0], wbuf[1]
            xs_hi[block(m), block(0)], xs_lo[block(m), block(0)] = split(pr * wr - pi * wi)
            xs_hi[block(m), block(1)], xs_lo[block(m), block(1)] = split(pr * wi + pi * wr)
        for m in (0, 1):
            y = dot3(xs_hi[block(m), :], xs_lo[block(m), :], b_hi[...], b_lo[...])
            for p in (0, 1):
                ls_hi[block(p), block(m)], ls_lo[block(p), block(m)] = split(y[:, block(p)])
        for p in (0, 1):
            fbuf[p] = dot3(a_hi[block(p), :], a_lo[block(p), :], ls_hi[...], ls_lo[...])
        intensity = sum(fbuf[p, :, block(m)] ** 2 for p in (0, 1) for m in (0, 1))
        factor = amps[batch].astype(F32) * lax.rsqrt(jnp.maximum(intensity, 0.1)) - 1.0
        for p in (0, 1):
            for m in (0, 1):
                ls_hi[block(p), block(m)], ls_lo[block(p), block(m)] = split(
                    fbuf[p, :, block(m)] * factor)
        for p in (0, 1):
            h = dot3(b_hi[block(p), :], b_lo[block(p), :], ls_hi[...], ls_lo[...])
            for m in (0, 1):
                xs_hi[block(m), block(p)], xs_lo[block(m), block(p)] = split(h[:, block(m)])
        for m in (0, 1):
            chi = dot3(xs_hi[block(m), :], xs_lo[block(m), :], a_hi[...], a_lo[...])
            cr, ci = chi[:, block(0)], chi[:, block(1)]
            wr, wi = wbuf[0], wbuf[1]
            pr, pi = probe[m, 0], probe[m, 1]
            grad_r, grad_i = wr * cr + wi * ci, wr * ci - wi * cr
            gor, goi = (pr * cr + pi * ci) * step, (pr * ci - pi * cr) * step
            if batch == 0:
                sbuf[2 * m], sbuf[2 * m + 1] = grad_r, grad_i
            else:
                sbuf[2 * m] += grad_r
                sbuf[2 * m + 1] += grad_i
            if m == 0:
                zbuf[0], zbuf[1] = gor, goi
            else:
                zbuf[0] += gor
                zbuf[1] += goi
            after_mode(m)

    def place(target, offset, col_start):
        height, total_lanes = target.shape[1:]
        row_table = one_hot((height, width), 0, offset)
        col_table = one_hot((width, total_lanes), 1, col_start)
        for p in (0, 1):
            target[p] = pick(zbuf[p], row_table, col_table)

    halo_arrives()
    fit(e0, pos[0], pos[1], 0, lambda m: None)
    place(gx, pos[0], pos[1])

    top, rest, late = slice(0, HALO), slice(HALO, tile_rows), slice(ODD_LOW, tile_rows)
    edge, mid = slice(0, HALO), slice(HALO, tile_cols)
    below = slice(odd_own, odd_own + HALO)
    s_rt, a_rt = remote(gx.at[:, top, halo], from_left.at[:, top], right, has_right, has_left)
    s_lt, a_lt = remote(gx.at[:, top, edge], from_right.at[:, top], left, has_left, has_right)
    s_rr, a_rr = remote(gx.at[:, rest, halo], from_left.at[:, rest], right, has_right, has_left)
    s_lr, a_lr = remote(gx.at[:, late, edge], from_right.at[:, late], left, has_left, has_right)
    s_um, a_um = remote(n1.at[:, top, mid], e1.at[:, below, mid], up, has_up, has_down)
    s_ue, a_ue = remote(n1.at[:, top, edge], e1.at[:, below, edge], up, has_up, has_down)
    s_uh, a_uh = remote(n1.at[:, top, halo], e1.at[:, below, halo], up, has_up, has_down)
    s_rt()
    s_lt()
    s_rr()
    s_lr()
    n1[:, top, mid] = e0[:, top, mid] + gx[:, top, mid]
    s_um()
    n1[:, rest, mid] = e0[:, rest, mid] + gx[:, rest, mid]
    inside = jnp.where(has_right, 1.0, 0.0).astype(F32)
    a_rt()
    n1[:, top, edge] = e0[:, top, edge] + gx[:, top, edge] + from_left[:, top]
    s_ue()
    a_lt()
    n1[:, top, halo] = (e0[:, top, halo] + gx[:, top, halo] + from_right[:, top]) * inside
    s_uh()
    a_rr()
    n1[:, rest, edge] = e0[:, rest, edge] + gx[:, rest, edge] + from_left[:, rest]
    a_lr()
    e1[:, 0:odd_own, 0:tile_cols] = n1[:, late, 0:tile_cols]
    e1[:, 0:odd_own, halo] = (e0[:, late, halo] + gx[:, late, halo] + from_right[:, late]) * inside
    a_um()
    a_ue()
    a_uh()

    core_copies = [
        remote(sbuf.at[2 * m + 1 - core], core_in.at[m], partner)
        for m in (0, 1) if reduce_here]

    def after_mode(m):
        if reduce_here:
            core_copies[m][0]()

    fit(e1, pos[2] - ODD_LOW, pos[3], 1, after_mode)
    place(g1, pos[2] - ODD_LOW, pos[3])

    s_sb, a_sb = remote(g1.at[:, below, halo], spill1.at[:, below], right, has_right, has_left)
    s_so, a_so = remote(g1.at[:, 0:odd_own, halo], spill1.at[:, 0:odd_own], right, has_right, has_left)
    s_dm, a_dm = remote(g1.at[:, below, mid], from_up.at[:, :, mid], down, has_down, has_up)
    s_de, a_de = remote(down_send, from_up.at[:, :, edge], down, has_down, has_up)
    s_sb()
    s_so()

    def relay():
        s_dm()
        a_sb()
        down_send[...] = g1[:, below, edge] + spill1[:, below]
        s_de()

    if reduce_here:
        part = width // n_row
        piece = part // n_zed
        row_base = row * part
        z_base = row_base + zed * piece
        row_copies, z_copies = [], []
        for m in (0, 1):
            core_copies[m][1]()
            tbuf[m] = sbuf[2 * m + core] + core_in[m]
            group = [
                remote(tbuf.at[m, pl.ds(pl.multiple_of(dev[0] * part, 8), part)], row_in.at[m, k], dev)
                for k, dev in enumerate(row_peers)]
            for start, _ in group:
                start()
            row_copies.append(group)
        relay()
        for m in (0, 1):
            total = tbuf[m, pl.ds(pl.multiple_of(row_base, 8), part)]
            for k, (_, arrive) in enumerate(row_copies[m]):
                arrive()
                total = total + row_in[m, k]
            ubuf[m] = total
            group = [
                remote(ubuf.at[m, pl.ds(pl.multiple_of(dev[1] // 2 * piece, 8), piece)], z_in.at[m, k], dev)
                for k, dev in enumerate(z_peers)]
            for start, _ in group:
                start()
            z_copies.append(group)
        z_back, row_back, core_back = [], [], []
        own = pl.ds(pl.multiple_of(z_base, 8), piece)
        for m in (0, 1):
            total = ubuf[m, pl.ds(pl.multiple_of(zed * piece, 8), piece)]
            for k, (_, arrive) in enumerate(z_copies[m]):
                arrive()
                total = total + z_in[m, k]
            gather[2 * m + core, own] = probe[m, core, own] + total * (1.0 / divisor)
            mine = gather.at[2 * m + core, own]
            group = [remote(mine, mine, dev) for dev in z_peers]
            for start, _ in group:
                start()
            z_back.append(group)
        for m in (0, 1):
            for _, arrive in z_back[m]:
                arrive()
            mine = gather.at[2 * m + core, pl.ds(pl.multiple_of(row_base, 8), part)]
            group = [remote(mine, mine, dev) for dev in row_peers]
            for start, _ in group:
                start()
            row_back.append(group)
    else:
        relay()

    a_so()
    a_dm()
    a_de()
    obj_out[:, top, :] = n1[:, top, 0:tile_cols] + from_up[...]
    obj_out[:, HALO:ODD_LOW, :] = n1[:, HALO:ODD_LOW, 0:tile_cols]
    obj_out[:, late, edge] = n1[:, late, edge] + (g1[:, 0:odd_own, edge] + spill1[:, 0:odd_own])
    obj_out[:, late, mid] = n1[:, late, mid] + g1[:, 0:odd_own, mid]

    if reduce_here:
        for m in (0, 1):
            for _, arrive in row_back[m]:
                arrive()
            mine = gather.at[2 * m + core]
            start, arrive = remote(mine, mine, partner)
            start()
            core_back.append(arrive)
        for m in (0, 1):
            core_back[m]()
            for p in (0, 1):
                probe_out[m, p] = gather[2 * m + p]
    else:
        for m in (0, 1):
            for p in (0, 1):
                probe_out[m, p] = sbuf[2 * m + p]

    for sends, copy in pending:
        if sends is None:
            copy.wait_send()
        else:
            pl.when(sends)(copy.wait_send)


def local(object_field, probe_modes, scan_positions, amplitudes):
    n_row, n_col = lax.axis_size("row"), lax.axis_size("col")
    width = probe_modes.shape[-1]
    _, tile_rows, tile_cols = object_field.shape
    batches = scan_positions.shape[2]
    divisor = math.sqrt(n_row * n_col * batches)
    lanes = tile_cols + HALO
    odd_rows = tile_rows - ODD_LOW + HALO
    n_zed = n_col // 2
    reduce_here = width % (n_row * n_zed * 8) == 0
    part = width // n_row
    piece = max(part // n_zed, 8)
    copies = 64 + 4 * (n_row + n_zed)
    vmem = pltpu.VMEM
    scratch = [
        vmem((2, tile_rows, lanes), F32),
        vmem((2, tile_rows, lanes), F32),
        vmem((2, tile_rows, lanes), F32),
        vmem((2, odd_rows, lanes), F32),
        vmem((2, odd_rows, lanes), F32),
        vmem((2, width, width), F32),
        vmem((2, tile_rows, HALO), F32),
        vmem((2, tile_rows, HALO), F32),
        vmem((2, odd_rows, HALO), F32),
        vmem((2, HALO, HALO), F32),
        vmem((2, HALO, tile_cols), F32),
    ]
    scratch += [vmem((2 * width, 2 * width), BF16) for _ in range(8)]
    scratch += [
        vmem((2, width, 2 * width), F32),
        vmem((2, width, width), F32),
        vmem((4, width, width), F32),
        vmem((2, width, width), F32),
        vmem((2, width, width), F32),
        vmem((2, n_row - 1, part, width), F32),
        vmem((2, part, width), F32),
        vmem((2, n_zed - 1, piece, width), F32),
        vmem((4, width, width), F32),
        pltpu.SemaphoreType.DMA((copies,)),
        pltpu.SemaphoreType.DMA((copies,)),
    ]
    whole = pl.BlockSpec(memory_space=pltpu.VMEM)
    object_out, probe_out = pl.pallas_call(
        functools.partial(kernel, n_row, n_col, reduce_here, divisor),
        out_shape=(
            jax.ShapeDtypeStruct(object_field.shape, F32),
            jax.ShapeDtypeStruct(probe_modes.shape, F32)),
        in_specs=[pl.BlockSpec(memory_space=pltpu.SMEM)] + [whole] * 4,
        out_specs=(whole, whole),
        scratch_shapes=scratch,
        compiler_params=pltpu.CompilerParams(
            collective_id=0, has_side_effects=True, vmem_limit_bytes=48 * 1024 * 1024),
        name="ptycho",
    )(
        scan_positions.reshape(-1), object_field, probe_modes,
        amplitudes.reshape(batches, width, width), jnp.asarray(dft_tables(width)))
    if not reduce_here:
        probe_out = probe_modes + lax.psum(probe_out, ("row", "col")) / divisor
    return object_out, probe_out


def solution(mesh):
    placed = (
        P(None, "row", "col"),
        P(),
        P("row", "col", None, None),
        P("row", "col", None, None, None),
    )
    return jax.shard_map(
        local, mesh=mesh, in_specs=placed, out_specs=(P(None, "row", "col"), P()), check_vma=False
    )
```

profile of v0, /device:TPU:1, one launch (start us, length us, event | category | flops | bytes accessed | tf_op | source)
XLA Modules:
  0.0 64.7 jit_solution(4412043827457431028)
XLA Ops:
  0.6 0.0 copy-start.4
  0.6 0.7 %copy-done.4 = s32[1,1,2,2]{3,2,1,0:T(2,128)S(1)} copy-done((s32[1,1,2,2]{3,2,1,0:T(2,128)S(1)}, s32[1,1,2,2]{3,2,1,0:T(2,128)}, u32[]{:S(2)}) %copy-start.4) | copy-done | bytes 40
  1.3 0.1 reshape.10.pos
  1.4 0.0 copy-start
  1.4 1.2 %copy-done = f32[2,2,256,256]{3,2,1,0:T(8,128)S(1)} copy-done((f32[2,2,256,256]{3,2,1,0:T(8,128)S(1)}, f32[2,2,256,256]{3,2,1,0:T(8,128)}, u32[]{:S(2)}) %copy-start) | copy-done | bytes 1048600
  2.6 0.0 copy-start.1
  2.6 1.1 %copy-done.1 = f32[2,384,256]{2,1,0:T(8,128)S(1)} copy-done((f32[2,384,256]{2,1,0:T(8,128)S(1)}, f32[2,384,256]{2,1,0:T(8,128)}, u32[]{:S(2)}) %copy-start.1) | copy-done | bytes 786456
  3.8 0.0 copy-start.2
  3.8 1.0 %copy-done.2 = bf16[4,256,256]{2,1,0:T(8,128)(2,1)S(1)} copy-done((bf16[4,256,256]{2,1,0:T(8,128)(2,1)S(1)}, bf16[4,256,256]{2,1,0:T(8,128)(2,1)}, u32[]{:S(2)}) %copy-start.2) | copy-done | bytes 524312
  4.8 0.0 copy-start.3
  4.8 0.9 %copy-done.3 = bf16[1,1,2,256,256]{4,3,2,1,0:T(8,128)(2,1)S(1)} copy-done((bf16[1,1,2,256,256]{4,3,2,1,0:T(8,128)(2,1)S(1)}, bf16[1,1,2,256,256]{4,3,2,1,0:T(8,128)(2,1)}, u32[]{:S(2)}) %copy-start.3) | copy-done | bytes 262168
  5.7 57.1 %ptycho.1 = (f32[2,384,256]{2,1,0:T(8,128)S(1)}, f32[2,2,256,256]{3,2,1,0:T(8,128)S(1)}) custom-call(s32[4]{0:T(128)S(1)} %reshape.10.pos, f32[2,384,256]{2,1,0:T(8,128)S(1)} %copy-done.1, f32[2,2,256,256]{3,2,1,0:T(8,128)S(1)} %copy-done, bf16[2,256,256]{2,1,0:T(8,128)(2,1)S(1)} %bitcast.1, bf16[4,256,256]{2,1,0:T(8,128)(2,1)S(1)} %copy-done.2), custom_call_target="tpu_custom_call" | custom-call | tf_op jit(solution)/shard_map/ptycho/pallas_call | solution.py:386
  62.9 0.9 %copy.9 = f32[2,384,256]{2,1,0:T(8,128)} copy(f32[2,384,256]{2,1,0:T(8,128)S(1)} %get-tuple-element.4) | data formatting | bytes 1572864
  63.8 1.0 %copy.10 = f32[2,2,256,256]{3,2,1,0:T(8,128)} copy(f32[2,2,256,256]{3,2,1,0:T(8,128)S(1)} %get-tuple-element.5) | data formatting | bytes 2097152
Async XLA Ops:
  0.6 0.7 %copy-start.4 = (s32[1,1,2,2]{3,2,1,0:T(2,128)S(1)}, s32[1,1,2,2]{3,2,1,0:T(2,128)}, u32[]{:S(2)}) copy-start(s32[1,1,2,2]{3,2,1,0:T(2,128)} %param.7) | copy-start | bytes 52
  1.4 1.2 %copy-start = (f32[2,2,256,256]{3,2,1,0:T(8,128)S(1)}, f32[2,2,256,256]{3,2,1,0:T(8,128)}, u32[]{:S(2)}) copy-start(f32[2,2,256,256]{3,2,1,0:T(8,128)} %probe.1) | copy-start | bytes 3145732
  2.6 1.1 %copy-start.1 = (f32[2,384,256]{2,1,0:T(8,128)S(1)}, f32[2,384,256]{2,1,0:T(8,128)}, u32[]{:S(2)}) copy-start(f32[2,384,256]{2,1,0:T(8,128)} %obj.1) | copy-start | bytes 2359300
  3.8 1.0 %copy-start.2 = (bf16[4,256,256]{2,1,0:T(8,128)(2,1)S(1)}, bf16[4,256,256]{2,1,0:T(8,128)(2,1)}, u32[]{:S(2)}) copy-start(bf16[4,256,256]{2,1,0:T(8,128)(2,1)} %constant.2.clone.tables) | copy-start | bytes 1572868
  4.8 0.9 %copy-start.3 = (bf16[1,1,2,256,256]{4,3,2,1,0:T(8,128)(2,1)S(1)}, bf16[1,1,2,256,256]{4,3,2,1,0:T(8,128)(2,1)}, u32[]{:S(2)}) copy-start(bf16[1,1,2,256,256]{4,3,2,1,0:T(8,128)(2,1)} %param.8) | copy-start | bytes 786436
where the time goes:
time: 65 us; the launch traced here: 64.7 us
  Pallas kernels  57.1 us (88%)
  local copies, waits for them, and re-layouts  6.95 us (11%)
  between operations  0.65 us (1%)
    pallas_call x1, Pallas kernels, local(): pl.pallas_call(functools.partial(kernel, n_row, n_col, reduce_here, divis...  57.1 us
    unnamed x12, local copies, waits for them, and re-layouts  6.87 us

commit v1 on v0

--- a/solution.py
+++ b/solution.py
@@ -40,7 +40,8 @@
 
 def kernel(
     n_row, n_col, reduce_here, divisor,
-    pos, obj, probe, amps, tables, obj_out, probe_out,
+    pos, obj, probe_in, amps_in, tables_in, obj_hbm, probe_hbm,
+    probe, amps, tables, obj_out, lsem,
     e0, gx, n1, e1, g1, zbuf, from_left, from_right, spill1, down_send, from_up,
     a_hi, a_lo, b_hi, b_lo, xs_hi, xs_lo, ls_hi, ls_lo, fbuf, wbuf,
     sbuf, core_in, tbuf, row_in, ubuf, z_in, gather, ssem, rsem,
@@ -86,6 +87,13 @@
 
         return start, arrive
 
+    fetches = [
+        pltpu.make_async_copy(src, dst, lsem.at[i])
+        for i, (src, dst) in enumerate((
+            (tables_in, tables), (obj, e0.at[:, :, 0:tile_cols]), (probe_in, probe), (amps_in, amps)))]
+    for fetch in fetches:
+        fetch.start()
+
     barrier = pltpu.get_barrier_semaphore()
     beside = (row, lax.rem(col + 2 * core - 1 + n_col, n_col))
     greeted = [partner, beside] + row_peers + z_peers
@@ -97,7 +105,7 @@
     start, halo_arrives = remote(obj.at[:, :, 0:HALO], e0.at[:, 0:tile_rows, halo], left, has_left, has_right)
     start()
 
-    e0[:, 0:tile_rows, 0:tile_cols] = obj[...]
+    fetches[0].wait()
     for hi, part in ((True, 0), (False, 1)):
         cosine, sine = tables[part], tables[2 + part]
         a, b = (a_hi, b_hi) if hi else (a_lo, b_lo)
@@ -108,6 +116,7 @@
         a[width:, 0:width] = -sine
         b[0:width, width:] = -sine
         b[width:, 0:width] = sine
+    fetches[2].wait()
     power = jnp.sum(
         jnp.sum(probe[0, 0] ** 2 + probe[0, 1] ** 2 + probe[1, 0] ** 2 + probe[1, 1] ** 2,
                 axis=0, keepdims=True), axis=1, keepdims=True) / (width * width)
@@ -173,21 +182,25 @@
         for m in (0, 1):
             chi = dot3(xs_hi[block(m), :], xs_lo[block(m), :], a_hi[...], a_lo[...])
             cr, ci = chi[:, block(0)], chi[:, block(1)]
-            wr, wi = wbuf[0], wbuf[1]
             pr, pi = probe[m, 0], probe[m, 1]
-            grad_r, grad_i = wr * cr + wi * ci, wr * ci - wi * cr
             gor, goi = (pr * cr + pi * ci) * step, (pr * ci - pi * cr) * step
-            if batch == 0:
-                sbuf[2 * m], sbuf[2 * m + 1] = grad_r, grad_i
-            else:
-                sbuf[2 * m] += grad_r
-                sbuf[2 * m + 1] += grad_i
             if m == 0:
                 zbuf[0], zbuf[1] = gor, goi
             else:
                 zbuf[0] += gor
                 zbuf[1] += goi
-            after_mode(m)
+            if batch == 0:
+                fbuf[m] = chi
+            else:
+                probe_terms(chi, m, True)
+                after_mode(m)
+
+    def probe_terms(chi, m, more):
+        cr, ci = chi[:, block(0)], chi[:, block(1)]
+        wr, wi = wbuf[0], wbuf[1]
+        terms = (wr * cr + wi * ci, wr * ci - wi * cr)
+        for p in (0, 1):
+            sbuf[2 * m + p] = sbuf[2 * m + p] + terms[p] if more else terms[p]
 
     def place(target, offset, col_start):
         height, total_lanes = target.shape[1:]
@@ -196,9 +209,11 @@
         for p in (0, 1):
             target[p] = pick(zbuf[p], row_table, col_table)
 
+    fetches[1].wait()
+    fetches[3].wait()
     halo_arrives()
-    fit(e0, pos[0], pos[1], 0, lambda m: None)
-    place(gx, pos[0], pos[1])
+    fit(e0, pos[0, 0, 0, 0], pos[0, 0, 0, 1], 0, lambda m: None)
+    place(gx, pos[0, 0, 0, 0], pos[0, 0, 0, 1])
 
     top, rest, late = slice(0, HALO), slice(HALO, tile_rows), slice(ODD_LOW, tile_rows)
     edge, mid = slice(0, HALO), slice(HALO, tile_cols)
@@ -216,6 +231,8 @@
     s_lr()
     n1[:, top, mid] = e0[:, top, mid] + gx[:, top, mid]
     s_um()
+    for m in (0, 1):
+        probe_terms(fbuf[m], m, False)
     n1[:, rest, mid] = e0[:, rest, mid] + gx[:, rest, mid]
     inside = jnp.where(has_right, 1.0, 0.0).astype(F32)
     a_rt()
@@ -241,8 +258,8 @@
         if reduce_here:
             core_copies[m][0]()
 
-    fit(e1, pos[2] - ODD_LOW, pos[3], 1, after_mode)
-    place(g1, pos[2] - ODD_LOW, pos[3])
+    fit(e1, pos[0, 0, 1, 0] - ODD_LOW, pos[0, 0, 1, 1], 1, after_mode)
+    place(g1, pos[0, 0, 1, 0] - ODD_LOW, pos[0, 0, 1, 1])
 
     s_sb, a_sb = remote(g1.at[:, below, halo], spill1.at[:, below], right, has_right, has_left)
     s_so, a_so = remote(g1.at[:, 0:odd_own, halo], spill1.at[:, 0:odd_own], right, has_right, has_left)
@@ -316,6 +333,8 @@
     obj_out[:, HALO:ODD_LOW, :] = n1[:, HALO:ODD_LOW, 0:tile_cols]
     obj_out[:, late, edge] = n1[:, late, edge] + (g1[:, 0:odd_own, edge] + spill1[:, 0:odd_own])
     obj_out[:, late, mid] = n1[:, late, mid] + g1[:, 0:odd_own, mid]
+    stores = [pltpu.make_async_copy(obj_out, obj_hbm, lsem.at[len(fetches)])]
+    stores[0].start()
 
     if reduce_here:
         for m in (0, 1):
@@ -327,13 +346,17 @@
             core_back.append(arrive)
         for m in (0, 1):
             core_back[m]()
-            for p in (0, 1):
-                probe_out[m, p] = gather[2 * m + p]
+            stores.append(pltpu.make_async_copy(
+                gather.at[pl.ds(2 * m, 2)], probe_hbm.at[m], lsem.at[len(fetches) + 1 + m]))
+            stores[-1].start()
     else:
         for m in (0, 1):
-            for p in (0, 1):
-                probe_out[m, p] = sbuf[2 * m + p]
-
+            stores.append(pltpu.make_async_copy(
+                sbuf.at[pl.ds(2 * m, 2)], probe_hbm.at[m], lsem.at[len(fetches) + 1 + m]))
+            stores[-1].start()
+
+    for store in stores:
+        store.wait()
     for sends, copy in pending:
         if sends is None:
             copy.wait_send()
@@ -356,6 +379,11 @@
     copies = 64 + 4 * (n_row + n_zed)
     vmem = pltpu.VMEM
     scratch = [
+        vmem(probe_modes.shape, F32),
+        vmem((batches, width, width), amplitudes.dtype),
+        vmem((4, width, width), BF16),
+        vmem(object_field.shape, F32),
+        pltpu.SemaphoreType.DMA((8,)),
         vmem((2, tile_rows, lanes), F32),
         vmem((2, tile_rows, lanes), F32),
         vmem((2, tile_rows, lanes), F32),
@@ -382,7 +410,7 @@
         pltpu.SemaphoreType.DMA((copies,)),
         pltpu.SemaphoreType.DMA((copies,)),
     ]
-    whole = pl.BlockSpec(memory_space=pltpu.VMEM)
+    whole = pl.BlockSpec(memory_space=pltpu.HBM)
     object_out, probe_out = pl.pallas_call(
         functools.partial(kernel, n_row, n_col, reduce_here, divisor),
         out_shape=(
@@ -392,10 +420,10 @@
         out_specs=(whole, whole),
         scratch_shapes=scratch,
         compiler_params=pltpu.CompilerParams(
-            collective_id=0, has_side_effects=True, vmem_limit_bytes=48 * 1024 * 1024),
+            collective_id=0, has_side_effects=True, vmem_limit_bytes=64 * 1024 * 1024 - 128 * 1024),
         name="ptycho",
     )(
-        scan_positions.reshape(-1), object_field, probe_modes,
+        scan_positions, object_field, probe_modes,
         amplitudes.reshape(batches, width, width), jnp.asarray(dft_tables(width)))
     if not reduce_here:
         probe_out = probe_modes + lax.psum(probe_out, ("row", "col")) / divisor

time: 65 us -> 61.9 us (0.952)
  local copies, waits for them, and re-layouts: 6.95 us -> 3.13 us
  Pallas kernels: 57.1 us -> 58 us
    unnamed x12 -> x4, local copies, waits for them, and re-layouts: 6.87 us -> 3.13 us
    pallas_call x1, Pallas kernels: 57.1 us -> 58 us  [local(): pl.pallas_call(functools.partial(kernel, n_row, n_col, reduce_here, divis...]
where the time goes in v1:
time: 61.9 us; the launch traced here: 61.7 us
  Pallas kernels  58 us (94%)
  local copies, waits for them, and re-layouts  3.13 us (5%)
  between operations  0.65 us (1%)
    pallas_call x1, Pallas kernels, local(): pl.pallas_call(functools.partial(kernel, n_row, n_col, reduce_here, divis...  58 us
    unnamed x4, local copies, waits for them, and re-layouts  3.13 us

profile of v1, /device:TPU:1, one launch (start us, length us, event | category | flops | bytes accessed | tf_op | source)
XLA Modules:
  0.0 61.7 jit_solution(9779025565917535761)
XLA Ops:
  0.6 58.0 %ptycho.1 = (f32[2,384,256]{2,1,0:T(8,128)}, f32[2,2,256,256]{3,2,1,0:T(8,128)}) custom-call(s32[1,1,2,2]{3,2,1,0:T(2,128)} %pos.1, f32[2,384,256]{2,1,0:T(8,128)} %obj.1, f32[2,2,256,256]{3,2,1,0:T(8,128)} %probe_in.1, bf16[2,256,256]{2,1,0:T(8,128)(2,1)} %bitcast.1, bf16[4,256,256]{2,1,0:T(8,128)(2,1)} %constant.2.clone.tables_in), custom_call_target="tpu_custom_call" | custom-call | tf_op jit(solution)/shard_map/ptycho/pallas_call | solution.py:414
  58.6 0.0 copy-start
  58.6 2.2 %copy.9 = f32[2,384,256]{2,1,0:T(8,128)} copy(f32[2,384,256]{2,1,0:T(8,128)} %get-tuple-element.4) | data formatting | bytes 1572864
  60.8 0.0 copy-done
  60.8 1.0 %copy.10 = f32[2,2,256,256]{3,2,1,0:T(8,128)} copy(f32[2,2,256,256]{3,2,1,0:T(8,128)S(1)} %copy-done) | data formatting | bytes 2097152
Async XLA Ops:
  58.6 2.2 %copy-start = (f32[2,2,256,256]{3,2,1,0:T(8,128)S(1)}, f32[2,2,256,256]{3,2,1,0:T(8,128)}, u32[]{:S(2)}) copy-start(f32[2,2,256,256]{3,2,1,0:T(8,128)} %get-tuple-element.5) | copy-start | bytes 3145732
